TPU v7x, 32 devices: a whole 2x2x4 slice. The times are simulated.
32 devices in a mesh: section: 2 (over core), tensor: 4 (over y, x), dp: 4 (over z).
Axes of the slice: x: 2, y: 2, z: 4, core: 2. Of those that a mesh axis runs over, the one named last changes fastest.
Arguments:
- enc_resid: bfloat16 [256, 16, 2048], P(('section', 'tensor'), 'dp'), parts along dimension 1, may hold values from -6 to 6
- enc_branch: bfloat16 [256, 16, 2048], P(('section', 'tensor'), 'dp'), parts along dimension 1, may hold values from -4 to 4
- enc_gain: float32 [2048], replicated, may hold values from 0.1 to 1.9
- dec_in: bfloat16 [16, 128, 2048], P('dp', 'tensor'), parts along dimension 0, may hold values from -6 to 6
- q_weight: bfloat16 [2, 2048, 2048], P('section', None, 'tensor'), may hold values from -0.125 to 0.125
- kv_weight: bfloat16 [2, 2048, 2, 2048], P('section', None, None, 'tensor'), may hold values from -0.125 to 0.125
- out_weight: bfloat16 [2, 2048, 2048], P('section', 'tensor'), may hold values from -0.75 to 0.75
- temps: float32 [2, 8], P('section', 'tensor'), may hold values from 4 to 16
- enc_lengths: int32 [16], P('dp'), parts along dimension 0, may hold values from 1 to 256, 768 in all
Outputs:
- section_out: bfloat16 [2, 16, 128, 2048], P('section', 'dp', 'tensor'), parts along dimension 1
There are 4 independent parts, one for each index of `dp`. A program takes and returns all parts, laid end to end along the dimension named above; an argument that names none is the same for every part. Nothing has to cross between parts.
Inputs may be any that keep to these rules, and one draw needn't show every extreme that they name: enc_lengths[m] is the number of unpadded encoder positions of sequence m; positions from it on are padding. Within each dp part (4 consecutive sequences), the lengths sum to 768 and one of them equals 256.
All inputs are finite; a program needn't handle non-finite values.
Results may differ from a plain program's by a relative error of at most 0.015.
Values may be sent and summed in bfloat16 or wider, within the bound.
A program may use at most 64 MiB of HBM per device.

v0:
```python
import jax
import jax.numpy as jnp
from jax import lax
from jax.sharding import PartitionSpec as P

HD = 256
L_ENC = 256


EPS = 1e-06


def shifted(value, axis, steps):
    count = lax.axis_size(axis)
    first, last = (max(0, -steps), min(count, count - steps))
    return lax.ppermute(value, axis, [(source, source + steps) for source in range(first, last)])


def head_norm(values, size):
    shaped = values.reshape(values.shape[:-1] + (values.shape[-1] // size, size))
    factor = lax.rsqrt(jnp.mean(shaped * shaped, axis=-1, keepdims=True) + EPS)
    return (shaped * factor).astype(jnp.bfloat16)


def encoder_norm(enc_resid, enc_branch, enc_gain):
    total = enc_resid.astype(jnp.float32) + enc_branch.astype(jnp.float32)
    factor = lax.rsqrt(jnp.mean(total * total, axis=-1, keepdims=True) + EPS)
    return (total * factor * enc_gain).astype(jnp.bfloat16)


def local(
    enc_resid, enc_branch, enc_gain, dec_in, q_weight, kv_weight, out_weight, temps, enc_lengths
):
    normed = encoder_norm(enc_resid, enc_branch, enc_gain)
    micro = dec_in.shape[0]
    local_rows = dec_in.shape[1]
    width = dec_in.shape[2]
    sections = lax.axis_size("section")
    section_id = lax.axis_index("section")
    kv_matrix = kv_weight[0].reshape(width, -1)
    inner = q_weight.shape[2]
    heads_here = inner // HD
    factor = temps[0] / HD
    positions = jnp.arange(L_ENC, dtype=jnp.int32)
    zero_index = jnp.int32(0)

    def query_piece(piece):
        return jnp.dot(piece, q_weight[0], preferred_element_type=jnp.float32)

    def run_tick(tick, carry):
        incoming, stored, cache = carry
        member = tick - section_id
        active = jnp.logical_and(member >= 0, member < micro)
        picked = jnp.clip(member, 0, micro - 1)
        own = lax.dynamic_index_in_dim(dec_in, picked, 0, keepdims=False)
        current = jnp.where(section_id == 0, own, incoming)
        query = query_piece(lax.all_gather(current, "tensor", axis=0, tiled=True))
        query_n = head_norm(query, HD)
        block = lax.dynamic_index_in_dim(cache, picked, 1, keepdims=False)
        keys_n = head_norm(block[:, :inner].astype(jnp.float32), HD)
        values = block[:, inner:].reshape(-1, heads_here, HD)
        scores = jnp.einsum("qhd,khd->hqk", query_n, keys_n, preferred_element_type=jnp.float32)
        scores = scores * factor[:, None, None]
        valid = positions < enc_lengths[picked]
        weights = jnp.where(valid[None, None, :], jnp.exp(scores), 0.0)
        probs = (weights / jnp.sum(weights, axis=-1, keepdims=True)).astype(jnp.bfloat16)
        attended = jnp.einsum("hqk,khd->qhd", probs, values, preferred_element_type=jnp.float32)
        attended = attended.astype(jnp.bfloat16).reshape(-1, inner)
        summed = lax.psum_scatter(
            jnp.dot(attended, out_weight[0], preferred_element_type=jnp.float32).astype(
                jnp.bfloat16
            ),
            "tensor",
            scatter_dimension=0,
            tiled=True,
        ).astype(jnp.float32)
        updated = (current.astype(jnp.float32) + summed).astype(jnp.bfloat16)
        written = lax.dynamic_update_slice(stored, updated[None], (picked, zero_index, zero_index))
        stored = jnp.where(active, written, stored)
        passed = shifted(updated, "section", 1)
        return (passed, stored, cache)

    first_in = jnp.zeros((local_rows, width), jnp.bfloat16)
    stored_init = jnp.zeros((micro, local_rows, width), jnp.bfloat16)
    piece = lax.all_gather(normed, ("section", "tensor"), axis=0, tiled=True)
    leading = piece.shape[:-1]
    flat = jnp.dot(piece.reshape(-1, width), kv_matrix, preferred_element_type=jnp.float32)
    full_cache = flat.astype(jnp.bfloat16).reshape(leading + (kv_matrix.shape[1],))
    carry = lax.fori_loop(0, micro + sections - 1, run_tick, (first_in, stored_init, full_cache))
    return carry[1][None]


def solution(mesh):
    return jax.shard_map(
        local,
        mesh=mesh,
        in_specs=(
            P(("section", "tensor"), "dp", None),
            P(("section", "tensor"), "dp", None),
            P(),
            P("dp", "tensor", None),
            P("section", None, "tensor"),
            P("section", None, None, "tensor"),
            P("section", "tensor", None),
            P("section", "tensor"),
            P("dp"),
        ),
        out_specs=P("section", "dp", "tensor", None),
        check_vma=False,
    )
```

profile of v0, /device:TPU:1, one launch (start us, length us, event | category | flops | bytes accessed | tf_op | source)
XLA Modules:
  0.0 315.5 jit_solution(12042079257613232116)
XLA Ops:
  6.5 1.7 multiply_reduce_fusion.1
  8.2 2.5 multiply_convert_fusion.2
  10.8 5.4 %copy.19 = bf16[256,8,2,512]{3,1,2,0:T(8,128)(2,1)} copy(bf16[256,8,2,512]{3,2,1,0:T(2,128)(2,1)} %bitcast.74) | data formatting | bytes 8388608
  16.1 2.9 copy.17
  19.1 31.0 %all-gather.2.cloned.1.call-done = bf16[256,4,2048]{2,1,0:T(4,128)(2,1)} async-done(((bf16[32,4,2048]{2,1,0:T(4,128)(2,1)}), bf16[256,4,2048]{2,1,0:T(4,128)(2,1)}) %all-gather.2.cloned.1.call-update) | async-done | bytes 4194320 | tf_op jit(solution)/shard_map/all_gather | solution.py:85
  50.2 6.9 %reshape.81 = bf16[1024,2048]{1,0:T(8,128)(2,1)} reshape(bf16[256,4,2048]{2,1,0:T(4,128)(2,1)} %all-gather.2.cloned.1.call-done) | data formatting | bytes 8388608 | tf_op jit(solution)/shard_map/reshape | solution.py:87
  57.1 9.3 %convolution_convert_fusion.2 = bf16[1024,1024]{1,0:T(8,128)(2,1)} fusion(bf16[1024,2048]{1,0:T(8,128)(2,1)} %reshape.81, bf16[2048,1024]{1,0:T(8,128)(2,1)} %bitcast.75), kind=kOutput, calls=%fused_computation.28 | convolution fusion | flops 4296015872 | bytes 10485760 | tf_op jit(solution)/shard_map/dot_general | solution.py:87
  66.4 4.1 %reshape.82 = bf16[256,4,1024]{2,1,0:T(4,128)(2,1)} reshape(bf16[1024,1024]{1,0:T(8,128)(2,1)} %convolution_convert_fusion.2) | data formatting | bytes 4194304 | tf_op jit(solution)/shard_map/reshape | solution.py:88
  70.5 4.3 %copy.16 = bf16[256,4,1024]{0,2,1:T(8,128)(2,1)} copy(bf16[256,4,1024]{2,1,0:T(4,128)(2,1)} %reshape.82) | data formatting | bytes 4194304
  74.9 233.0 %while.17 = (s32[]{:T(128)}, bf16[32,2048]{1,0:T(8,128)(2,1)S(1)}, bf16[4,32,2048]{2,1,0:T(8,128)(2,1)S(1)}, pred[]{:T(512)}, s32[]{:T(128)}, /*index=5*/bf16[4,...) while((s32[]{:T(128)}, bf16[32,2048]{1,0:T(8,128)(2,1)S(1)}, ...), condition=%wide.region_6.7_spmd.clone, body=%wide.region_1.6_spmd.clone.sunk | while | flops 606012928 | bytes 13644604 | solution.py:89
  75.0 1.1 dynamic-slice_bitcast_fusion.2
  76.2 0.9 bitcast_select_fusion.3
  77.1 8.7 %all_gather.14 = bf16[128,2048]{1,0:T(8,128)(2,1)S(1)} all-gather(bf16[32,2048]{1,0:T(8,128)(2,1)S(1)} %bitcast_select_fusion.3), channel_id=1, replica_groups=mesh['section'=2,'tensor'=4,'dp'=4] {'tensor'}, dimensions={0}, use_global_device_ids=true | all-gather | bytes 655360 | tf_op jit(solution)/shard_map/while/body/eval_jaxpr/all_gather | solution.py:57
  88.5 2.9 convolution_convert_fusion.6
  91.4 25.9 %reduce-scatter.2.cloned.1.call-done = bf16[32,2048]{1,0:T(8,128)(2,1)} async-done(((bf16[128,2048]{1,0:T(8,128)(2,1)}), bf16[32,2048]{1,0:T(8,128)(2,1)}) %reduce-scatter.2.cloned.1.call-update) | async-done | bytes 131088 | tf_op jit(solution)/shard_map/while/body/eval_jaxpr/reduce_scatter | solution.py:69
  117.2 1.0 fusion.42
  118.2 1.3 collective-permute-start
  119.5 1.9 collective-permute-done
  121.5 1.1 dynamic-slice_bitcast_fusion.2
  122.6 0.9 bitcast_select_fusion.3
  123.6 8.9 %all_gather.14 = bf16[128,2048]{1,0:T(8,128)(2,1)S(1)} all-gather(bf16[32,2048]{1,0:T(8,128)(2,1)S(1)} %bitcast_select_fusion.3), channel_id=1, replica_groups=mesh['section'=2,'tensor'=4,'dp'=4] {'tensor'}, dimensions={0}, use_global_device_ids=true | all-gather | bytes 655360 | tf_op jit(solution)/shard_map/while/body/eval_jaxpr/all_gather | solution.py:57
  135.2 2.9 convolution_convert_fusion.6
  138.1 25.7 %reduce-scatter.2.cloned.1.call-done = bf16[32,2048]{1,0:T(8,128)(2,1)} async-done(((bf16[128,2048]{1,0:T(8,128)(2,1)}), bf16[32,2048]{1,0:T(8,128)(2,1)}) %reduce-scatter.2.cloned.1.call-update) | async-done | bytes 131088 | tf_op jit(solution)/shard_map/while/body/eval_jaxpr/reduce_scatter | solution.py:69
  163.8 1.0 fusion.42
  164.8 1.3 collective-permute-start
  166.1 1.9 collective-permute-done
  168.0 1.1 dynamic-slice_bitcast_fusion.2
  169.2 0.9 bitcast_select_fusion.3
  170.2 8.9 %all_gather.14 = bf16[128,2048]{1,0:T(8,128)(2,1)S(1)} all-gather(bf16[32,2048]{1,0:T(8,128)(2,1)S(1)} %bitcast_select_fusion.3), channel_id=1, replica_groups=mesh['section'=2,'tensor'=4,'dp'=4] {'tensor'}, dimensions={0}, use_global_device_ids=true | all-gather | bytes 655360 | tf_op jit(solution)/shard_map/while/body/eval_jaxpr/all_gather | solution.py:57
  181.8 2.9 convolution_convert_fusion.6
  184.7 25.7 %reduce-scatter.2.cloned.1.call-done = bf16[32,2048]{1,0:T(8,128)(2,1)} async-done(((bf16[128,2048]{1,0:T(8,128)(2,1)}), bf16[32,2048]{1,0:T(8,128)(2,1)}) %reduce-scatter.2.cloned.1.call-update) | async-done | bytes 131088 | tf_op jit(solution)/shard_map/while/body/eval_jaxpr/reduce_scatter | solution.py:69
  210.4 1.0 fusion.42
  211.4 1.3 collective-permute-start
  212.7 1.9 collective-permute-done
  214.6 1.1 dynamic-slice_bitcast_fusion.2
  216.8 8.9 %all_gather.14 = bf16[128,2048]{1,0:T(8,128)(2,1)S(1)} all-gather(bf16[32,2048]{1,0:T(8,128)(2,1)S(1)} %bitcast_select_fusion.3), channel_id=1, replica_groups=mesh['section'=2,'tensor'=4,'dp'=4] {'tensor'}, dimensions={0}, use_global_device_ids=true | all-gather | bytes 655360 | tf_op jit(solution)/shard_map/while/body/eval_jaxpr/all_gather | solution.py:57
  228.4 2.9 convolution_convert_fusion.6
  231.3 25.7 %reduce-scatter.2.cloned.1.call-done = bf16[32,2048]{1,0:T(8,128)(2,1)} async-done(((bf16[128,2048]{1,0:T(8,128)(2,1)}), bf16[32,2048]{1,0:T(8,128)(2,1)}) %reduce-scatter.2.cloned.1.call-update) | async-done | bytes 131088 | tf_op jit(solution)/shard_map/while/body/eval_jaxpr/reduce_scatter | solution.py:69
  257.0 1.0 fusion.42
  258.0 1.3 collective-permute-start
  259.3 1.9 collective-permute-done
  261.2 1.1 dynamic-slice_bitcast_fusion.2
  263.4 8.9 %all_gather.14 = bf16[128,2048]{1,0:T(8,128)(2,1)S(1)} all-gather(bf16[32,2048]{1,0:T(8,128)(2,1)S(1)} %bitcast_select_fusion.3), channel_id=1, replica_groups=mesh['section'=2,'tensor'=4,'dp'=4] {'tensor'}, dimensions={0}, use_global_device_ids=true | all-gather | bytes 655360 | tf_op jit(solution)/shard_map/while/body/eval_jaxpr/all_gather | solution.py:57
  275.0 2.9 convolution_convert_fusion.6
  277.9 25.7 %reduce-scatter.2.cloned.1.call-done = bf16[32,2048]{1,0:T(8,128)(2,1)} async-done(((bf16[128,2048]{1,0:T(8,128)(2,1)}), bf16[32,2048]{1,0:T(8,128)(2,1)}) %reduce-scatter.2.cloned.1.call-update) | async-done | bytes 131088 | tf_op jit(solution)/shard_map/while/body/eval_jaxpr/reduce_scatter | solution.py:69
  303.6 1.0 fusion.42
  304.6 1.3 collective-permute-start
  305.9 1.9 collective-permute-done
  (69 shorter events, 17.0 us)
Async XLA Ops:
  6.5 43.6 %all-gather.2.cloned.1.call-start = ((), (), s32[]{:S(2)}) async-start(), calls=%async_computation.1 | async-start | bytes 4718592 | tf_op jit(solution)/shard_map/all_gather | solution.py:85
  16.1 2.9 copy-start.1
  70.5 4.4 %copy-start.2 = (s32[4]{0:T(128)S(1)}, s32[4]{0:T(128)}, u32[]{:S(2)}) copy-start(s32[4]{0:T(128)} %param.19) | copy-start | bytes 52
  74.9 42.4 %reduce-scatter.2.cloned.1.call-start = ((), (), s32[]{:S(2)}) async-start(), calls=%async_computation.2 | async-start | bytes 655360 | tf_op jit(solution)/shard_map/while/body/eval_jaxpr/reduce_scatter | solution.py:69
  118.2 3.2 %collective-permute-start = (bf16[32,2048]{1,0:T(8,128)(2,1)S(1)}, bf16[32,2048]{1,0:T(8,128)(2,1)S(1)}, u32[]{:S(2)}, u32[]{:S(2)}) collective-permute-start(bf16[32,2048]{1,0:T(8,128)(2,1)S(1)} %get-tuple-element.401), channel_id=1, source_target_pairs={{0,16},{1,17},{2,18},{3,19},{4,20},{5,21},{6,22},{7,23},{8,24},{9,... | collective-permute-start | bytes 393224 | tf_op jit(solution)/shard_map/while/body/eval_jaxpr/ppermute | solution.py:16
  121.4 42.4 %reduce-scatter.2.cloned.1.call-start = ((), (), s32[]{:S(2)}) async-start(), calls=%async_computation.2 | async-start | bytes 655360 | tf_op jit(solution)/shard_map/while/body/eval_jaxpr/reduce_scatter | solution.py:69
  164.8 3.2 %collective-permute-start = (bf16[32,2048]{1,0:T(8,128)(2,1)S(1)}, bf16[32,2048]{1,0:T(8,128)(2,1)S(1)}, u32[]{:S(2)}, u32[]{:S(2)}) collective-permute-start(bf16[32,2048]{1,0:T(8,128)(2,1)S(1)} %get-tuple-element.401), channel_id=1, source_target_pairs={{0,16},{1,17},{2,18},{3,19},{4,20},{5,21},{6,22},{7,23},{8,24},{9,... | collective-permute-start | bytes 393224 | tf_op jit(solution)/shard_map/while/body/eval_jaxpr/ppermute | solution.py:16
  168.0 42.4 %reduce-scatter.2.cloned.1.call-start = ((), (), s32[]{:S(2)}) async-start(), calls=%async_computation.2 | async-start | bytes 655360 | tf_op jit(solution)/shard_map/while/body/eval_jaxpr/reduce_scatter | solution.py:69
  211.4 3.2 %collective-permute-start = (bf16[32,2048]{1,0:T(8,128)(2,1)S(1)}, bf16[32,2048]{1,0:T(8,128)(2,1)S(1)}, u32[]{:S(2)}, u32[]{:S(2)}) collective-permute-start(bf16[32,2048]{1,0:T(8,128)(2,1)S(1)} %get-tuple-element.401), channel_id=1, source_target_pairs={{0,16},{1,17},{2,18},{3,19},{4,20},{5,21},{6,22},{7,23},{8,24},{9,... | collective-permute-start | bytes 393224 | tf_op jit(solution)/shard_map/while/body/eval_jaxpr/ppermute | solution.py:16
  214.6 42.4 %reduce-scatter.2.cloned.1.call-start = ((), (), s32[]{:S(2)}) async-start(), calls=%async_computation.2 | async-start | bytes 655360 | tf_op jit(solution)/shard_map/while/body/eval_jaxpr/reduce_scatter | solution.py:69
  258.0 3.2 %collective-permute-start = (bf16[32,2048]{1,0:T(8,128)(2,1)S(1)}, bf16[32,2048]{1,0:T(8,128)(2,1)S(1)}, u32[]{:S(2)}, u32[]{:S(2)}) collective-permute-start(bf16[32,2048]{1,0:T(8,128)(2,1)S(1)} %get-tuple-element.401), channel_id=1, source_target_pairs={{0,16},{1,17},{2,18},{3,19},{4,20},{5,21},{6,22},{7,23},{8,24},{9,... | collective-permute-start | bytes 393224 | tf_op jit(solution)/shard_map/while/body/eval_jaxpr/ppermute | solution.py:16
  261.2 42.4 %reduce-scatter.2.cloned.1.call-start = ((), (), s32[]{:S(2)}) async-start(), calls=%async_computation.2 | async-start | bytes 655360 | tf_op jit(solution)/shard_map/while/body/eval_jaxpr/reduce_scatter | solution.py:69
  304.6 3.2 %collective-permute-start = (bf16[32,2048]{1,0:T(8,128)(2,1)S(1)}, bf16[32,2048]{1,0:T(8,128)(2,1)S(1)}, u32[]{:S(2)}, u32[]{:S(2)}) collective-permute-start(bf16[32,2048]{1,0:T(8,128)(2,1)S(1)} %get-tuple-element.401), channel_id=1, source_target_pairs={{0,16},{1,17},{2,18},{3,19},{4,20},{5,21},{6,22},{7,23},{8,24},{9,... | collective-permute-start | bytes 393224 | tf_op jit(solution)/shard_map/while/body/eval_jaxpr/ppermute | solution.py:16
  307.8 0.8 copy-start
Sparse Core Ops, SparseCore 0:
  10.9 39.2 all-gather.1
  91.5 25.6 reduce-scatter.1
  138.3 25.5 reduce-scatter.1
  184.8 25.5 reduce-scatter.1
  231.5 25.5 reduce-scatter.1
  278.0 25.5 reduce-scatter.1
where the time goes:
time: 317 us; the launch traced here: 315 us
  waiting for transfers between devices  169 us (53%)
  blocking collectives  44.3 us (14%)
  local copies, waits for them, and re-layouts  33 us (10%)
  matrix products  31 us (10%)
  other arithmetic  17.3 us (5%)
  between operations  13.4 us (4%)
  starting transfers between devices  6.51 us (2%)
    reduce_scatter x5, waiting for transfers between devices, run_tick(): lax.psum_scatter(jnp.dot(attended, out_weight[0], preferred_element_type=...  129 us
    all_gather x5, blocking collectives, run_tick(): query = query_piece(lax.all_gather(current, 'tensor', axis=0, tiled=True))  44.3 us
    all_gather x1, waiting for transfers between devices, local(): piece = lax.all_gather(normed, ('section', 'tensor'), axis=0, tiled=True)  31 us
    dot_general x5, matrix products, run_tick(): jnp.dot(attended, out_weight[0], preferred_element_type=jnp.float32)  14.3 us
    unnamed x9, local copies, waits for them, and re-layouts  13.4 us
    ppermute x5, waiting for transfers between devices, shifted(): lax.ppermute(value, axis, [(source, source + steps) for source in range(f...  9.69 us
    dot_general x1, matrix products, local(): jnp.dot(piece.reshape(-1, width), kv_matrix, preferred_element_type=jnp.f...  9.3 us
    reshape x1, local copies, waits for them, and re-layouts, local(): piece.reshape(-1, width)  6.9 us
  transfers between devices with their start and end apart: 11, of which 11 were waited for; matrix products, arithmetic and copies ran while one was open for 3% of the time, Pallas kernels for 0%

commit v1 on v0

v1 whole, which is shorter than its diff:
```python
import functools

import jax
import jax.numpy as jnp
from jax import lax
from jax.experimental import pallas as pl
from jax.experimental.pallas import tpu as pltpu
from jax.sharding import PartitionSpec as P

HD = 256
EPS = 1e-06
HALVES = 2
MESH = pl.DeviceIdType.MESH


def head_norm(values):
    factor = lax.rsqrt(jnp.mean(values * values, axis=-1, keepdims=True) + EPS)
    return (values * factor).astype(jnp.bfloat16)


def landed(ref, sem):
    pltpu.make_async_copy(ref, ref, sem).wait()


def kernel(
    sections, span, normed, dec, wq_hbm, wkv_hbm, wo_hbm, temps, lens, out,
    enc, wq, wkv, wo, kv, xg, part, pr, xs,
    own_sem, weight_sem, out_sem, enc_send, enc_recv, half_recv,
    x_own, x_first_send, x_next_send, x_recv, part_send, part_recv,
):
    section = lax.axis_index("section")
    tensor = lax.axis_index("tensor")
    micro, tensors, rows, width = xg.shape
    inner = wq.shape[1]
    heads = inner // HD
    per_half = micro // HALVES
    positions = tensors * sections * span
    half_width = width // 2
    peers = [tensor, tensor + 1 - 2 * lax.rem(tensor, 2), lax.rem(tensor + 2, 4), 3 - tensor]

    def remote(src, dst, send_sem, recv_sem, to_section, to_tensor):
        return pltpu.make_async_remote_copy(
            src_ref=src, dst_ref=dst, send_sem=send_sem, recv_sem=recv_sem,
            device_id={"section": to_section, "tensor": to_tensor}, device_id_type=MESH,
        )

    others = [lax.rem(section + k, sections) for k in range(1, sections)]

    for h in range(HALVES):
        pltpu.make_async_copy(normed.at[h], enc.at[h, 0, section], own_sem.at[h]).start()

    @pl.when(section == 0)
    def _():
        for m in range(micro):
            pltpu.make_async_copy(dec.at[m], xg.at[m, 0], x_own.at[m]).start()

    weights = [
        pltpu.make_async_copy(src, dst, weight_sem.at[i])
        for i, (src, dst) in enumerate(((wkv_hbm, wkv), (wq_hbm, wq), (wo_hbm, wo)))
    ]
    for copy in weights:
        copy.start()

    barrier = pltpu.get_barrier_semaphore()
    for to_section in [section] + others:
        for d in range(tensors):
            if d == 0 and to_section is section:
                continue
            pl.semaphore_signal(
                barrier, inc=1, device_id={"section": to_section, "tensor": peers[d]}, device_id_type=MESH
            )
    pl.semaphore_wait(barrier, sections * tensors - 1)

    started = []

    def send_block(h, d, place, copies):
        for k, other in enumerate(others):
            copies.append(
                remote(
                    enc.at[h, d, section], enc.at[h, d, section],
                    enc_send.at[h, place + k], enc_recv.at[h, d, section], other, tensor,
                )
            )

    def begin(copies):
        for copy in copies:
            copy.start()
        started.extend(copies)

    def send_own(h):
        landed(enc.at[h, 0, section], own_sem.at[h])
        copies = [
            remote(
                enc.at[h, 0, section], enc.at[h, d, section],
                enc_send.at[h, d - 1], enc_recv.at[h, d, section], section, peers[d],
            )
            for d in (1, 2)
        ]
        send_block(h, 0, 4, copies)
        begin(copies)

    def pass_on(h, d):
        landed(enc.at[h, d, section], enc_recv.at[h, d, section])
        columns = pl.ds((d - 1) * half_width, half_width)
        copies = [
            remote(
                enc.at[h, d, section, :, columns], enc.at[h, 3, section, :, columns],
                enc_send.at[h, 1 + d], half_recv.at[h, d - 1], section, peers[3 - d],
            )
        ]
        send_block(h, d, 4 + d * (sections - 1), copies)
        begin(copies)

    def pass_last(h):
        for i in range(2):
            landed(enc.at[h, 3, section, :, pl.ds(i * half_width, half_width)], half_recv.at[h, i])
        copies = []
        send_block(h, 3, 4 + 3 * (sections - 1), copies)
        begin(copies)

    def from_others(h):
        for d in range(tensors):
            for other in others:
                landed(enc.at[h, d, other], enc_recv.at[h, d, other])

    def first_copy(m, d):
        return remote(
            xg.at[m, 0], xg.at[m, d], x_first_send.at[m, d], x_recv.at[m, d], section, peers[d]
        )

    def send_first(which):
        @pl.when(section == 0)
        def _():
            for m in which:
                landed(xg.at[m, 0], x_own.at[m])
                for d in range(1, tensors):
                    first_copy(m, d).start()

    def project(h):
        block = enc.shape[3]

        @pl.loop(0, heads)
        def _(head):
            at_key = pl.multiple_of(head * HD, HD)
            at_value = pl.multiple_of(inner + head * HD, HD)
            joined = enc[h].reshape(tensors * sections * block, width)
            keys = jnp.dot(joined, wkv[:, pl.ds(at_key, HD)], preferred_element_type=jnp.float32)
            keys = head_norm(keys.astype(jnp.bfloat16).astype(jnp.float32)).astype(kv.dtype)
            values = jnp.dot(joined, wkv[:, pl.ds(at_value, HD)], preferred_element_type=jnp.float32)
            values = values.astype(jnp.bfloat16).astype(kv.dtype)
            for i in range(tensors * sections):
                for j in range(per_half):
                    place = (i * per_half + j) * span
                    target = (h * per_half + j, pl.ds(i * span, span))
                    kv[target + (pl.ds(at_key, HD),)] = keys[place:place + span]
                    kv[target + (pl.ds(at_value, HD),)] = values[place:place + span]

    row = lax.broadcasted_iota(jnp.int32, (1, positions), 1)
    distance = row // (sections * span)
    sender = jnp.where(
        distance == 0, peers[0], jnp.where(distance == 1, peers[1], jnp.where(distance == 2, peers[2], peers[3]))
    )
    place_of = ((row // span) % sections * tensors + sender) * span + row % span

    def part_copy(m, d):
        return remote(
            part.at[m, d], pr.at[m, d], part_send.at[m, d], part_recv.at[m, d], section, peers[d]
        )

    def next_copy(m, d):
        return remote(
            xs.at[m], xg.at[m, d], x_next_send.at[m, d], x_recv.at[m, d], section + 1, peers[d]
        )

    def attend(m):
        current = xg[m].reshape(tensors * rows, width)
        query = jnp.dot(current, wq[...], preferred_element_type=jnp.float32)
        valid = place_of < lens[m]
        attended = []
        for head in range(heads):
            at = head * HD
            query_n = head_norm(query[:, at:at + HD])
            keys_n = kv[m, :, at:at + HD].astype(jnp.bfloat16)
            values = kv[m, :, inner + at:inner + at + HD].astype(jnp.bfloat16)
            scores = lax.dot_general(
                query_n, keys_n, (((1,), (1,)), ((), ())), preferred_element_type=jnp.float32
            )
            unscaled = jnp.where(valid, jnp.exp(scores * (temps[0, head] / HD)), 0.0)
            probs = (unscaled / jnp.sum(unscaled, axis=-1, keepdims=True)).astype(jnp.bfloat16)
            attended.append(
                jnp.dot(probs, values, preferred_element_type=jnp.float32).astype(jnp.bfloat16)
            )
        attended = jnp.concatenate(attended, axis=1)
        partial = jnp.dot(attended, wo[...], preferred_element_type=jnp.float32).astype(jnp.bfloat16)
        part[m] = partial.reshape(tensors, rows, width)
        for d in range(1, tensors):
            part_copy(m, d).start()

    def finish(m):
        total = part[m, 0].astype(jnp.float32)
        for d in range(1, tensors):
            landed(pr.at[m, d], part_recv.at[m, d])
            total = total + pr[m, d].astype(jnp.float32)
        xs[m] = (xg[m, 0].astype(jnp.float32) + total).astype(jnp.bfloat16)

        @pl.when(section < sections - 1)
        def _():
            for d in range(tensors):
                next_copy(m, d).start()

        pltpu.make_async_copy(xs.at[m], out.at[m], out_sem.at[m]).start()

    send_own(0)
    send_first((0,))
    pass_on(0, 1)
    pass_on(0, 2)
    send_own(1)
    send_first(range(1, micro))
    pass_last(0)
    from_others(0)
    weights[0].wait()
    project(0)
    pass_on(1, 1)
    pass_on(1, 2)
    pass_last(1)
    from_others(1)
    project(1)
    weights[1].wait()
    weights[2].wait()

    @pl.loop(0, micro + 1)
    def _(step):
        @pl.when(step < micro)
        def _():
            @pl.when(section > 0)
            def _():
                landed(xg.at[step, 0], x_recv.at[step, 0])

            for d in range(1, tensors):
                landed(xg.at[step, d], x_recv.at[step, d])
            attend(step)

        @pl.when(step > 0)
        def _():
            finish(step - 1)

    for copy in started:
        copy.wait_send()

    @pl.loop(0, micro)
    def _(m):
        for d in range(1, tensors):
            part_copy(m, d).wait_send()
        pltpu.make_async_copy(xs.at[m], out.at[m], out_sem.at[m]).wait()

    @pl.when(section == 0)
    def _():
        @pl.loop(0, micro)
        def _(m):
            for d in range(1, tensors):
                first_copy(m, d).wait_send()

    @pl.when(section < sections - 1)
    def _():
        @pl.loop(0, micro)
        def _(m):
            for d in range(tensors):
                next_copy(m, d).wait_send()


def encoder_norm(enc_resid, enc_branch, enc_gain):
    total = enc_resid.astype(jnp.float32) + enc_branch.astype(jnp.float32)
    factor = lax.rsqrt(jnp.mean(total * total, axis=-1, keepdims=True) + EPS)
    return (total * factor * enc_gain).astype(jnp.bfloat16)


def local(
    enc_resid, enc_branch, enc_gain, dec_in, q_weight, kv_weight, out_weight, temps, enc_lengths
):
    sections = lax.axis_size("section")
    tensors = lax.axis_size("tensor")
    span, micro, width = enc_resid.shape
    rows = dec_in.shape[1]
    inner = q_weight.shape[2]
    block = micro // HALVES * span
    normed = encoder_norm(enc_resid, enc_branch, enc_gain)
    normed = normed.transpose(1, 0, 2).reshape(HALVES, block, width)
    kv_matrix = kv_weight[0].reshape(width, 2 * inner)
    positions = tensors * sections * span
    cache_type = jnp.bfloat16 if span % 16 == 0 else jnp.float32
    any_space = pl.BlockSpec(memory_space=pl.ANY)
    smem = pl.BlockSpec(memory_space=pltpu.SMEM)
    dma = pltpu.SemaphoreType.DMA
    bf16 = jnp.bfloat16
    tokens = micro * tensors * rows
    flops = 2 * micro * positions * width * 2 * inner + 4 * tokens * width * inner
    stored = pl.pallas_call(
        functools.partial(kernel, sections, span),
        out_shape=jax.ShapeDtypeStruct((micro, rows, width), bf16),
        in_specs=[any_space] * 5 + [smem] * 2,
        out_specs=any_space,
        scratch_shapes=[
            pltpu.VMEM((HALVES, tensors, sections, block, width), bf16),
            pltpu.VMEM((width, inner), bf16),
            pltpu.VMEM((width, 2 * inner), bf16),
            pltpu.VMEM((inner, width), bf16),
            pltpu.VMEM((micro, positions, 2 * inner), cache_type),
            pltpu.VMEM((micro, tensors, rows, width), bf16),
            pltpu.VMEM((micro, tensors, rows, width), bf16),
            pltpu.VMEM((micro, tensors, rows, width), bf16),
            pltpu.VMEM((micro, rows, width), bf16),
            dma((HALVES,)),
            dma((3,)),
            dma((micro,)),
            dma((HALVES, 4 + tensors * (sections - 1))),
            dma((HALVES, tensors, sections)),
            dma((HALVES, 2)),
            dma((micro,)),
            dma((micro, tensors)),
            dma((micro, tensors)),
            dma((micro, tensors)),
            dma((micro, tensors)),
            dma((micro, tensors)),
        ],
        compiler_params=pltpu.CompilerParams(
            collective_id=0, has_side_effects=True, vmem_limit_bytes=48 * 1024 * 1024
        ),
        cost_estimate=pl.CostEstimate(flops=flops, bytes_accessed=12 << 20, transcendentals=0),
    )(normed, dec_in, q_weight[0], kv_matrix, out_weight[0], temps, enc_lengths)
    return stored[None]


def solution(mesh):
    return jax.shard_map(
        local,
        mesh=mesh,
        in_specs=(
            P(("section", "tensor"), "dp", None),
            P(("section", "tensor"), "dp", None),
            P(),
            P("dp", "tensor", None),
            P("section", None, "tensor"),
            P("section", None, None, "tensor"),
            P("section", "tensor", None),
            P("section", "tensor"),
            P("dp"),
        ),
        out_specs=P("section", "dp", "tensor", None),
        check_vma=False,
    )
```

time: 317 us -> 89.3 us (0.28)
  waiting for transfers between devices: 169 us -> 0 us
  Pallas kernels: 0 us -> 79 us
  blocking collectives: 44.3 us -> 0 us
  matrix products: 31 us -> 0 us
  local copies, waits for them, and re-layouts: 33 us -> 6.6 us
  other arithmetic: 17.3 us -> 3.42 us
  between operations: 13.4 us -> 0.08 us
  starting transfers between devices: 6.51 us -> 0 us
    reduce_scatter x5 -> x0, waiting for transfers between devices: 129 us -> none  [run_tick(): lax.psum_scatter(jnp.dot(attended, out_weight[0], preferred_element_type=...]
    pallas_call x0 -> x1, Pallas kernels: none -> 79 us  [local(): pl.pallas_call(functools.partial(kernel, sections, span), out_shape=jax.S...]
    all_gather x5 -> x0, blocking collectives: 44.3 us -> none  [run_tick(): query = query_piece(lax.all_gather(current, 'tensor', axis=0, tiled=True))]
    all_gather x1 -> x0, waiting for transfers between devices: 31 us -> none  [local(): piece = lax.all_gather(normed, ('section', 'tensor'), axis=0, tiled=True)]
    dot_general x21 -> x0, matrix products: 31 us -> none  [the longest x5 14.3 us: run_tick(): jnp.dot(attended, out_weight[0], preferred_element_type=jnp.float32)]
    reshape x2 -> x0, local copies, waits for them, and re-layouts: 11 us -> none  [the longest x1 6.9 us: local(): piece.reshape(-1, width)]
    ppermute x5 -> x0, waiting for transfers between devices: 9.69 us -> none  [shifted(): lax.ppermute(value, axis, [(source, source + steps) for source in range(f...]
    select_n x10 -> x0, other arithmetic: 9.41 us -> none  [the longest x5 4.79 us: run_tick(): stored = jnp.where(active, written, stored)]
  transfers between devices with their start and end apart: 11 -> 0, of which waited for: 11 -> 0; matrix products, arithmetic and copies ran while one was open for 3% -> 0% of each run, Pallas kernels for 0% -> 0%
where the time goes in v1:
time: 89.3 us; the launch traced here: 89.1 us
  Pallas kernels  79 us (88%)
  local copies, waits for them, and re-layouts  6.6 us (7%)
  other arithmetic  3.42 us (4%)
    pallas_call x1, Pallas kernels, local(): pl.pallas_call(functools.partial(kernel, sections, span), out_shape=jax.S...  79 us
    unnamed x12, local copies, waits for them, and re-layouts  6.3 us

profile of v1, /device:TPU:1, one launch (start us, length us, event | category | flops | bytes accessed | tf_op | source)
XLA Modules:
  0.0 89.1 jit_solution(4564631106023786756)
XLA Ops:
  0.0 1.7 %multiply_reduce_fusion = f32[32,4]{1,0:T(8,128)S(1)} fusion(bf16[32,4,2048]{2,1,0:T(4,128)(2,1)} %param.10, bf16[32,4,2048]{2,1,0:T(4,128)(2,1)} %param.9), kind=kLoop, calls=%fused_computation.1 | loop fusion | flops 1310592 | bytes 1049088 | tf_op jit(solution)/shard_map/reduce_sum | solution.py:273
  1.7 1.7 %fusion = bf16[4,32,2048]{2,0,1:T(4,128)(2,1)S(1)} fusion(bf16[32,4,2048]{2,1,0:T(4,128)(2,1)} %param.10, bf16[32,4,2048]{2,1,0:T(4,128)(2,1)} %param.9, f32[2048]{0:T(1024)} %param.11, f32[32,4]{1,0:T(8,128)S(1)} %add_rsqrt_fusion), kind=kLoop, calls=%fused_computation.3 | loop fusion | flops 1572864 | bytes 1581568 | tf_op jit(solution)/shard_map/transpose | solution.py:287
  3.4 0.3 copy.15
  3.7 0.0 copy-start
  3.7 0.0 copy-start.1
  3.8 0.0 copy-start.2
  3.8 0.0 copy-start.3
  3.8 0.0 copy-start.4
  3.8 5.5 %copy.16 = bf16[256,8,2,512]{3,1,2,0:T(8,128)(2,1)} copy(bf16[256,8,2,512]{3,2,1,0:T(2,128)(2,1)} %bitcast.13) | data formatting | bytes 8388608
  9.3 0.0 copy-done
  9.3 0.0 copy-done.1
  9.3 0.0 copy-done.2
  9.3 0.0 copy-done.3
  9.3 0.0 copy-done.4
  9.3 79.0 %shard_map.91 = bf16[4,32,2048]{2,1,0:T(8,128)(2,1)S(1)} custom-call(bf16[2,64,2048]{2,1,0:T(8,128)(2,1)S(1)} %bitcast.9, bf16[4,32,2048]{2,1,0:T(8,128)(2,1)S(1)} %copy-done.2, bf16[2048,512]{1,0:T(8,128)(2,1)S(1)} %bitcast.11, bf16[2048,1024]{1,0:T(8,128)(2,1)} %bitcast.14, bf16[512,2048]{1,0:T(8,128)(2,1)S(1)} %bitcast.12, f32[1,2]{1,0:T(1,128)S(1)} %copy-done.3, ...), custom_call_target="tpu_custom_call" | custom-call | flops 6442450944 | bytes 12582912 | tf_op jit(solution)/shard_map/pallas_call | solution.py:297
  88.3 0.8 copy.19
  (1 shorter events, 0.0 us)
Async XLA Ops:
  3.7 5.5 %copy-start = (bf16[1,2048,512]{2,1,0:T(8,128)(2,1)S(1)}, bf16[1,2048,512]{2,1,0:T(8,128)(2,1)}, u32[]{:S(2)}) copy-start(bf16[1,2048,512]{2,1,0:T(8,128)(2,1)} %param.13) | copy-start | bytes 6291460
  3.7 5.5 %copy-start.1 = (bf16[1,512,2048]{2,1,0:T(8,128)(2,1)S(1)}, bf16[1,512,2048]{2,1,0:T(8,128)(2,1)}, u32[]{:S(2)}) copy-start(bf16[1,512,2048]{2,1,0:T(8,128)(2,1)} %param.15) | copy-start | bytes 6291460
  3.8 5.5 %copy-start.2 = (bf16[4,32,2048]{2,1,0:T(8,128)(2,1)S(1)}, bf16[4,32,2048]{2,1,0:T(8,128)(2,1)}, u32[]{:S(2)}) copy-start(bf16[4,32,2048]{2,1,0:T(8,128)(2,1)} %dec.1) | copy-start | bytes 1572868
  3.8 5.5 %copy-start.3 = (f32[1,2]{1,0:T(1,128)S(1)}, f32[1,2]{1,0:T(1,128)}, u32[]{:S(2)}) copy-start(f32[1,2]{1,0:T(1,128)} %temps.1) | copy-start | bytes 28
  3.8 5.5 %copy-start.4 = (s32[4]{0:T(128)S(1)}, s32[4]{0:T(128)}, u32[]{:S(2)}) copy-start(s32[4]{0:T(128)} %lens.1) | copy-start | bytes 52

commit v2 on v1

--- a/solution.py
+++ b/solution.py
@@ -23,14 +23,15 @@
 
 
 def kernel(
-    sections, span, normed, dec, wq_hbm, wkv_hbm, wo_hbm, temps, lens, out,
-    enc, wq, wkv, wo, kv, xg, part, pr, xs,
-    own_sem, weight_sem, out_sem, enc_send, enc_recv, half_recv,
+    sections, resid_hbm, branch_hbm, gain, dec, wq_hbm, wkv_hbm, wo_hbm, temps, lens, out,
+    resid, branch, raw, enc, wq, wkv, wo, kv, xg, part, pr, xs,
+    load_sem, weight_sem, out_sem, enc_send, enc_recv, half_recv,
     x_own, x_first_send, x_next_send, x_recv, part_send, part_recv,
 ):
     section = lax.axis_index("section")
     tensor = lax.axis_index("tensor")
     micro, tensors, rows, width = xg.shape
+    span = resid.shape[0]
     inner = wq.shape[1]
     heads = inner // HD
     per_half = micro // HALVES
@@ -46,8 +47,12 @@
 
     others = [lax.rem(section + k, sections) for k in range(1, sections)]
 
-    for h in range(HALVES):
-        pltpu.make_async_copy(normed.at[h], enc.at[h, 0, section], own_sem.at[h]).start()
+    loads = [
+        pltpu.make_async_copy(resid_hbm, resid, load_sem.at[0]),
+        pltpu.make_async_copy(branch_hbm, branch, load_sem.at[1]),
+    ]
+    for copy in loads:
+        copy.start()
 
     @pl.when(section == 0)
     def _():
@@ -56,7 +61,7 @@
 
     weights = [
         pltpu.make_async_copy(src, dst, weight_sem.at[i])
-        for i, (src, dst) in enumerate(((wkv_hbm, wkv), (wq_hbm, wq), (wo_hbm, wo)))
+        for i, (src, dst) in enumerate(((wkv_hbm, raw), (wq_hbm, wq), (wo_hbm, wo)))
     ]
     for copy in weights:
         copy.start()
@@ -69,6 +74,18 @@
             pl.semaphore_signal(
                 barrier, inc=1, device_id={"section": to_section, "tensor": peers[d]}, device_id_type=MESH
             )
+
+    for copy in loads:
+        copy.wait()
+    chunk = min(span, 16)
+    for first in range(0, span, chunk):
+        total = resid[first:first + chunk].astype(jnp.float32) + branch[first:first + chunk].astype(jnp.float32)
+        factor = lax.rsqrt(jnp.mean(total * total, axis=-1, keepdims=True) + EPS)
+        normed = total * factor * gain[...].reshape(1, 1, width)
+        for m in range(micro):
+            at = m % per_half * span + first
+            enc[m // per_half, 0, section, at:at + chunk] = normed[:, m, :].astype(jnp.bfloat16)
+
     pl.semaphore_wait(barrier, sections * tensors - 1)
 
     started = []
@@ -88,7 +105,6 @@
         started.extend(copies)
 
     def send_own(h):
-        landed(enc.at[h, 0, section], own_sem.at[h])
         copies = [
             remote(
                 enc.at[h, 0, section], enc.at[h, d, section],
@@ -210,39 +226,66 @@
 
         pltpu.make_async_copy(xs.at[m], out.at[m], out_sem.at[m]).start()
 
+    def step(m):
+        @pl.when(section > 0)
+        def _():
+            landed(xg.at[m, 0], x_recv.at[m, 0])
+
+        for d in range(1, tensors):
+            landed(xg.at[m, d], x_recv.at[m, d])
+        attend(m)
+
+    def split_weights():
+        deep = 256
+
+        @pl.loop(0, width // deep)
+        def _(i):
+            features = pl.ds(pl.multiple_of(i * deep, deep), deep)
+            both = raw[features]
+            wkv[features, :inner] = both[:, 0, :]
+            wkv[features, inner:] = both[:, 1, :]
+
+    def in_first(work, *which):
+        @pl.when(section == 0)
+        def _():
+            for m in which:
+                work(m)
+
     send_own(0)
     send_first((0,))
+    weights[0].wait()
+    split_weights()
     pass_on(0, 1)
     pass_on(0, 2)
     send_own(1)
-    send_first(range(1, micro))
+    send_first((1,))
     pass_last(0)
     from_others(0)
-    weights[0].wait()
     project(0)
+    weights[1].wait()
+    weights[2].wait()
+    in_first(step, 0)
     pass_on(1, 1)
     pass_on(1, 2)
+    send_first(range(2, micro))
+    in_first(step, 1)
     pass_last(1)
+    in_first(finish, 0)
     from_others(1)
     project(1)
-    weights[1].wait()
-    weights[2].wait()
+    in_first(finish, 1)
+
+    done = jnp.where(section == 0, 2, 0)
 
     @pl.loop(0, micro + 1)
-    def _(step):
-        @pl.when(step < micro)
-        def _():
-            @pl.when(section > 0)
-            def _():
-                landed(xg.at[step, 0], x_recv.at[step, 0])
-
-            for d in range(1, tensors):
-                landed(xg.at[step, d], x_recv.at[step, d])
-            attend(step)
-
-        @pl.when(step > 0)
-        def _():
-            finish(step - 1)
+    def _(now):
+        @pl.when(jnp.logical_and(now >= done, now < micro))
+        def _():
+            step(now)
+
+        @pl.when(now > done)
+        def _():
+            finish(now - 1)
 
     for copy in started:
         copy.wait_send()
@@ -266,12 +309,6 @@
         def _(m):
             for d in range(tensors):
                 next_copy(m, d).wait_send()
-
-
-def encoder_norm(enc_resid, enc_branch, enc_gain):
-    total = enc_resid.astype(jnp.float32) + enc_branch.astype(jnp.float32)
-    factor = lax.rsqrt(jnp.mean(total * total, axis=-1, keepdims=True) + EPS)
-    return (total * factor * enc_gain).astype(jnp.bfloat16)
 
 
 def local(
@@ -283,23 +320,24 @@
     rows = dec_in.shape[1]
     inner = q_weight.shape[2]
     block = micro // HALVES * span
-    normed = encoder_norm(enc_resid, enc_branch, enc_gain)
-    normed = normed.transpose(1, 0, 2).reshape(HALVES, block, width)
-    kv_matrix = kv_weight[0].reshape(width, 2 * inner)
     positions = tensors * sections * span
     cache_type = jnp.bfloat16 if span % 16 == 0 else jnp.float32
     any_space = pl.BlockSpec(memory_space=pl.ANY)
+    vmem = pl.BlockSpec(memory_space=pltpu.VMEM)
     smem = pl.BlockSpec(memory_space=pltpu.SMEM)
     dma = pltpu.SemaphoreType.DMA
     bf16 = jnp.bfloat16
     tokens = micro * tensors * rows
     flops = 2 * micro * positions * width * 2 * inner + 4 * tokens * width * inner
     stored = pl.pallas_call(
-        functools.partial(kernel, sections, span),
+        functools.partial(kernel, sections),
         out_shape=jax.ShapeDtypeStruct((micro, rows, width), bf16),
-        in_specs=[any_space] * 5 + [smem] * 2,
+        in_specs=[any_space] * 2 + [vmem] + [any_space] * 4 + [smem] * 2,
         out_specs=any_space,
         scratch_shapes=[
+            pltpu.VMEM((span, micro, width), bf16),
+            pltpu.VMEM((span, micro, width), bf16),
+            pltpu.VMEM((width, 2, inner), bf16),
             pltpu.VMEM((HALVES, tensors, sections, block, width), bf16),
             pltpu.VMEM((width, inner), bf16),
             pltpu.VMEM((width, 2 * inner), bf16),
@@ -309,7 +347,7 @@
             pltpu.VMEM((micro, tensors, rows, width), bf16),
             pltpu.VMEM((micro, tensors, rows, width), bf16),
             pltpu.VMEM((micro, rows, width), bf16),
-            dma((HALVES,)),
+            dma((2,)),
             dma((3,)),
             dma((micro,)),
             dma((HALVES, 4 + tensors * (sections - 1))),
@@ -326,7 +364,10 @@
             collective_id=0, has_side_effects=True, vmem_limit_bytes=48 * 1024 * 1024
         ),
         cost_estimate=pl.CostEstimate(flops=flops, bytes_accessed=12 << 20, transcendentals=0),
-    )(normed, dec_in, q_weight[0], kv_matrix, out_weight[0], temps, enc_lengths)
+    )(
+        enc_resid, enc_branch, enc_gain.reshape(1, width), dec_in,
+        q_weight[0], kv_weight[0], out_weight[0], temps, enc_lengths,
+    )
     return stored[None]
 
 

time: 89.3 us -> 79.7 us (0.89)
  Pallas kernels: 79 us -> 71.9 us
  other arithmetic: 3.42 us -> 0 us
  local copies, waits for them, and re-layouts: 6.6 us -> 7.52 us
    pallas_call x1, Pallas kernels: 79 us -> 71.9 us  [local(): pl.pallas_call(functools.partial(kernel, sections), out_shape=jax.ShapeDt...]
    transpose x1 -> x0, other arithmetic: 1.73 us -> none  [local(): normed = normed.transpose(1, 0, 2).reshape(HALVES, block, width)]
    reduce_sum x1 -> x0, other arithmetic: 1.68 us -> none  [encoder_norm(): factor = lax.rsqrt(jnp.mean(total * total, axis=-1, keepdims=True) + EPS)]
    unnamed x12 -> x15, local copies, waits for them, and re-layouts: 6.3 us -> 7.52 us
where the time goes in v2:
time: 79.7 us; the launch traced here: 79.4 us
  Pallas kernels  71.9 us (90%)
  local copies, waits for them, and re-layouts  7.52 us (9%)
    pallas_call x1, Pallas kernels, local(): pl.pallas_call(functools.partial(kernel, sections), out_shape=jax.ShapeDt...  71.9 us
    unnamed x15, local copies, waits for them, and re-layouts  7.52 us

profile of v2, /device:TPU:1, one launch (start us, length us, event | category | flops | bytes accessed | tf_op | source)
XLA Modules:
  0.0 79.4 jit_solution(4532117829927750095)
XLA Ops:
  0.0 0.0 copy-start
  0.0 1.6 %copy-done = bf16[1,2048,512]{2,1,0:T(8,128)(2,1)S(1)} copy-done((bf16[1,2048,512]{2,1,0:T(8,128)(2,1)S(1)}, bf16[1,2048,512]{2,1,0:T(8,128)(2,1)}, u32[]{:S(2)}) %copy-start) | copy-done | bytes 2097176
  1.6 0.0 copy-start.1
  1.6 1.0 %copy-done.1 = bf16[32,4,2048]{2,1,0:T(4,128)(2,1)S(1)} copy-done((bf16[32,4,2048]{2,1,0:T(4,128)(2,1)S(1)}, bf16[32,4,2048]{2,1,0:T(4,128)(2,1)}, u32[]{:S(2)}) %copy-start.1) | copy-done | bytes 524312
  2.6 0.0 copy-start.2
  2.6 1.0 %copy-done.2 = bf16[32,4,2048]{2,1,0:T(4,128)(2,1)S(1)} copy-done((bf16[32,4,2048]{2,1,0:T(4,128)(2,1)S(1)}, bf16[32,4,2048]{2,1,0:T(4,128)(2,1)}, u32[]{:S(2)}) %copy-start.2) | copy-done | bytes 524312
  3.7 0.0 copy-start.3
  3.7 1.0 %copy-done.3 = bf16[4,32,2048]{2,1,0:T(8,128)(2,1)S(1)} copy-done((bf16[4,32,2048]{2,1,0:T(8,128)(2,1)S(1)}, bf16[4,32,2048]{2,1,0:T(8,128)(2,1)}, u32[]{:S(2)}) %copy-start.3) | copy-done | bytes 524312
  4.7 0.0 copy-start.4
  4.7 0.7 copy-done.4
  5.4 0.0 copy-start.5
  5.4 0.7 copy-done.5
  6.1 0.0 copy-start.6
  6.1 0.7 copy-done.6
  6.7 71.9 %shard_map.91 = bf16[4,32,2048]{2,1,0:T(8,128)(2,1)S(1)} custom-call(bf16[32,4,2048]{2,1,0:T(4,128)(2,1)S(1)} %copy-done.1, bf16[32,4,2048]{2,1,0:T(4,128)(2,1)S(1)} %copy-done.2, f32[1,2048]{1,0:T(1,128)S(1)} %bitcast.7, bf16[4,32,2048]{2,1,0:T(8,128)(2,1)S(1)} %copy-done.3, bf16[2048,512]{1,0:T(8,128)(2,1)S(1)} %bitcast.6, bf16[2048,2,512]{2,1,0:T(2,128)(2,1)} %bitcast.8, ...), custom_call_target="tpu_custom_call" | custom-call | flops 6442450944 | bytes 12582912 | tf_op jit(solution)/shard_map/pallas_call | solution.py:332
  78.6 0.8 %copy.11 = bf16[1,4,32,2048]{3,2,1,0:T(8,128)(2,1)} copy(bf16[1,4,32,2048]{3,2,1,0:T(8,128)(2,1)S(1)} %bitcast.5) | data formatting | bytes 1048576
Async XLA Ops:
  0.0 1.6 %copy-start = (bf16[1,2048,512]{2,1,0:T(8,128)(2,1)S(1)}, bf16[1,2048,512]{2,1,0:T(8,128)(2,1)}, u32[]{:S(2)}) copy-start(bf16[1,2048,512]{2,1,0:T(8,128)(2,1)} %param.13) | copy-start | bytes 6291460
  1.6 1.0 %copy-start.1 = (bf16[32,4,2048]{2,1,0:T(4,128)(2,1)S(1)}, bf16[32,4,2048]{2,1,0:T(4,128)(2,1)}, u32[]{:S(2)}) copy-start(bf16[32,4,2048]{2,1,0:T(4,128)(2,1)} %resid_hbm.1) | copy-start | bytes 1572868
  2.6 1.0 %copy-start.2 = (bf16[32,4,2048]{2,1,0:T(4,128)(2,1)S(1)}, bf16[32,4,2048]{2,1,0:T(4,128)(2,1)}, u32[]{:S(2)}) copy-start(bf16[32,4,2048]{2,1,0:T(4,128)(2,1)} %branch_hbm.1) | copy-start | bytes 1572868
  3.7 1.0 %copy-start.3 = (bf16[4,32,2048]{2,1,0:T(8,128)(2,1)S(1)}, bf16[4,32,2048]{2,1,0:T(8,128)(2,1)}, u32[]{:S(2)}) copy-start(bf16[4,32,2048]{2,1,0:T(8,128)(2,1)} %dec.1) | copy-start | bytes 1572868
  4.7 0.7 copy-start.4
  5.4 0.7 copy-start.5
  6.1 0.7 copy-start.6

commit v3 on v2

--- a/solution.py
+++ b/solution.py
@@ -26,7 +26,7 @@
     sections, resid_hbm, branch_hbm, gain, dec, wq_hbm, wkv_hbm, wo_hbm, temps, lens, out,
     resid, branch, raw, enc, wq, wkv, wo, kv, xg, part, pr, xs,
     load_sem, weight_sem, out_sem, enc_send, enc_recv, half_recv,
-    x_own, x_first_send, x_next_send, x_recv, part_send, part_recv,
+    x_own, x_first_send, x_next_send, x_recv, x_pass_send, x_half_recv, part_send, part_recv,
 ):
     section = lax.axis_index("section")
     tensor = lax.axis_index("tensor")
@@ -149,7 +149,7 @@
         def _():
             for m in which:
                 landed(xg.at[m, 0], x_own.at[m])
-                for d in range(1, tensors):
+                for d in (1, 2):
                     first_copy(m, d).start()
 
     def project(h):
@@ -188,6 +188,18 @@
             xs.at[m], xg.at[m, d], x_next_send.at[m, d], x_recv.at[m, d], section + 1, peers[d]
         )
 
+    def pass_copy(m, d):
+        columns = pl.ds((d - 1) * half_width, half_width)
+        return remote(
+            xg.at[m, d, :, columns], xg.at[m, 3, :, columns],
+            x_pass_send.at[m, d - 1], x_half_recv.at[m, d - 1], section, peers[3 - d],
+        )
+
+    def relay(m):
+        for d in (1, 2):
+            landed(xg.at[m, d], x_recv.at[m, d])
+            pass_copy(m, d).start()
+
     def attend(m):
         current = xg[m].reshape(tensors * rows, width)
         query = jnp.dot(current, wq[...], preferred_element_type=jnp.float32)
@@ -229,10 +241,14 @@
     def step(m):
         @pl.when(section > 0)
         def _():
-            landed(xg.at[m, 0], x_recv.at[m, 0])
-
-        for d in range(1, tensors):
-            landed(xg.at[m, d], x_recv.at[m, d])
+            for d in range(tensors):
+                landed(xg.at[m, d], x_recv.at[m, d])
+
+        @pl.when(section == 0)
+        def _():
+            for i in range(2):
+                landed(xg.at[m, 3, :, pl.ds(i * half_width, half_width)], x_half_recv.at[m, i])
+
         attend(m)
 
     def split_weights():
@@ -257,6 +273,7 @@
     split_weights()
     pass_on(0, 1)
     pass_on(0, 2)
+    in_first(relay, 0)
     send_own(1)
     send_first((1,))
     pass_last(0)
@@ -267,11 +284,13 @@
     in_first(step, 0)
     pass_on(1, 1)
     pass_on(1, 2)
+    in_first(relay, 1)
     send_first(range(2, micro))
     in_first(step, 1)
     pass_last(1)
     in_first(finish, 0)
     from_others(1)
+    in_first(relay, *range(2, micro))
     project(1)
     in_first(finish, 1)
 
@@ -300,8 +319,9 @@
     def _():
         @pl.loop(0, micro)
         def _(m):
-            for d in range(1, tensors):
+            for d in (1, 2):
                 first_copy(m, d).wait_send()
+                pass_copy(m, d).wait_send()
 
     @pl.when(section < sections - 1)
     def _():
@@ -357,11 +377,13 @@
             dma((micro, tensors)),
             dma((micro, tensors)),
             dma((micro, tensors)),
+            dma((micro, 2)),
+            dma((micro, 2)),
             dma((micro, tensors)),
             dma((micro, tensors)),
         ],
         compiler_params=pltpu.CompilerParams(
-            collective_id=0, has_side_effects=True, vmem_limit_bytes=48 * 1024 * 1024
+            collective_id=0, has_side_effects=True, vmem_limit_bytes=60 * 1024 * 1024
         ),
         cost_estimate=pl.CostEstimate(flops=flops, bytes_accessed=12 << 20, transcendentals=0),
     )(

time: 79.7 us -> 76.7 us (0.962)
  local copies, waits for them, and re-layouts: 7.52 us -> 1.88 us
  Pallas kernels: 71.9 us -> 74.6 us
    unnamed x15 -> x1, local copies, waits for them, and re-layouts: 7.52 us -> 1.88 us
    pallas_call x1, Pallas kernels: 71.9 us -> 74.6 us  [local(): pl.pallas_call(functools.partial(kernel, sections), out_shape=jax.ShapeDt...]
where the time goes in v3:
time: 76.7 us; the launch traced here: 76.5 us
  Pallas kernels  74.6 us (97%)
  local copies, waits for them, and re-layouts  1.88 us (2%)
    pallas_call x1, Pallas kernels, local(): pl.pallas_call(functools.partial(kernel, sections), out_shape=jax.ShapeDt...  74.6 us
    unnamed x1, local copies, waits for them, and re-layouts  1.88 us

profile of v3, /device:TPU:1, one launch (start us, length us, event | category | flops | bytes accessed | tf_op | source)
XLA Modules:
  0.0 76.5 jit_solution(2650937038073643867)
XLA Ops:
  0.0 74.6 %shard_map.91 = bf16[4,32,2048]{2,1,0:T(8,128)(2,1)} custom-call(bf16[32,4,2048]{2,1,0:T(4,128)(2,1)} %resid_hbm.1, bf16[32,4,2048]{2,1,0:T(4,128)(2,1)} %branch_hbm.1, f32[1,2048]{1,0:T(1,128)} %bitcast.9, bf16[4,32,2048]{2,1,0:T(8,128)(2,1)} %dec.1, bf16[2048,512]{1,0:T(8,128)(2,1)} %bitcast.7, bf16[2048,2,512]{2,1,0:T(2,128)(2,1)} %bitcast.6, ...), custom_call_target="tpu_custom_call" | custom-call | flops 6442450944 | bytes 12582912 | tf_op jit(solution)/shard_map/pallas_call | solution.py:352
  74.6 1.9 %copy.11 = bf16[1,4,32,2048]{3,2,1,0:T(8,128)(2,1)} copy(bf16[1,4,32,2048]{3,2,1,0:T(8,128)(2,1)} %bitcast.5) | data formatting | bytes 1048576

commit v4 on v3

--- a/solution.py
+++ b/solution.py
@@ -221,7 +221,7 @@
         attended = jnp.concatenate(attended, axis=1)
         partial = jnp.dot(attended, wo[...], preferred_element_type=jnp.float32).astype(jnp.bfloat16)
         part[m] = partial.reshape(tensors, rows, width)
-        for d in range(1, tensors):
+        for d in (3, 1, 2):
             part_copy(m, d).start()
 
     def finish(m):
@@ -233,7 +233,7 @@
 
         @pl.when(section < sections - 1)
         def _():
-            for d in range(tensors):
+            for d in (3, 1, 2, 0):
                 next_copy(m, d).start()
 
         pltpu.make_async_copy(xs.at[m], out.at[m], out_sem.at[m]).start()
@@ -288,11 +288,10 @@
     send_first(range(2, micro))
     in_first(step, 1)
     pass_last(1)
-    in_first(finish, 0)
+    in_first(finish, 0, 1)
     from_others(1)
     in_first(relay, *range(2, micro))
     project(1)
-    in_first(finish, 1)
 
     done = jnp.where(section == 0, 2, 0)
 

time: 76.7 us -> 75.9 us (0.990)
  Pallas kernels: 74.6 us -> 73.8 us
    pallas_call x1, Pallas kernels: 74.6 us -> 73.8 us  [local(): pl.pallas_call(functools.partial(kernel, sections), out_shape=jax.ShapeDt...]
where the time goes in v4:
time: 75.9 us; the launch traced here: 75.7 us
  Pallas kernels  73.8 us (97%)
  local copies, waits for them, and re-layouts  1.88 us (2%)
    pallas_call x1, Pallas kernels, local(): pl.pallas_call(functools.partial(kernel, sections), out_shape=jax.ShapeDt...  73.8 us
    unnamed x1, local copies, waits for them, and re-layouts  1.88 us

profile of v4, /device:TPU:1, one launch (start us, length us, event | category | flops | bytes accessed | tf_op | source)
XLA Modules:
  0.0 75.7 jit_solution(8890421469744947594)
XLA Ops:
  0.0 73.8 %shard_map.91 = bf16[4,32,2048]{2,1,0:T(8,128)(2,1)} custom-call(bf16[32,4,2048]{2,1,0:T(4,128)(2,1)} %resid_hbm.1, bf16[32,4,2048]{2,1,0:T(4,128)(2,1)} %branch_hbm.1, f32[1,2048]{1,0:T(1,128)} %bitcast.9, bf16[4,32,2048]{2,1,0:T(8,128)(2,1)} %dec.1, bf16[2048,512]{1,0:T(8,128)(2,1)} %bitcast.7, bf16[2048,2,512]{2,1,0:T(2,128)(2,1)} %bitcast.6, ...), custom_call_target="tpu_custom_call" | custom-call | flops 6442450944 | bytes 12582912 | tf_op jit(solution)/shard_map/pallas_call | solution.py:351
  73.8 1.9 %copy.11 = bf16[1,4,32,2048]{3,2,1,0:T(8,128)(2,1)} copy(bf16[1,4,32,2048]{3,2,1,0:T(8,128)(2,1)} %bitcast.5) | data formatting | bytes 1048576
